TPU v7x, 32 devices: a whole 2x2x4 slice. The times are simulated.
32 devices in a mesh: rec: 4 (over y, core), tract: 8 (over z, x).
Axes of the slice: x: 2, y: 2, z: 4, core: 2. Of those that a mesh axis runs over, the one named last changes fastest.
Arguments:
- rep_weights: float32 [80, 131072], P(None, ('rec', 'tract')), may hold values from 0.5 to 2
- covariate_codes: int32 [5, 131072], P(None, ('rec', 'tract')), may hold values from 0 to 15
- tract_of: int32 [131072, 1], P(('rec', 'tract')), may hold values from 0 to 7; in each aligned block of 4096 rows (0 to 4095, 4096 to 8191, ...) at most 1536 rows name the same one
- log_income: bfloat16 [131072], P(('rec', 'tract')), may hold values from -5 to 5
- controls: float32 [64], replicated, may hold values from 7782 to 10240
- threshold_grid: int32 [2048], replicated, may hold values from 0 to 4095
Outputs:
- calibrated: float32 [80, 131072], P(None, ('rec', 'tract'))
- income_tables: float32 [8, 80, 2048], P('tract', None, 'rec')
Inputs may be any that keep to these rules, and one draw needn't show every extreme that they name: `tract_of`: among the 4096 persons of one device at most 1536 share a tract; in some aligned blocks of 4096 persons one tract has exactly 1536.
All inputs are finite; a program needn't handle non-finite values.
Results may differ from a plain program's by a relative error of at most 0.0003.
Values may be sent and summed in bfloat16 or wider, within the bound.
A program may use at most 128 MiB of HBM per device.

v0:
```python
import math
import jax
import jax.numpy as jnp
from jax import lax
from jax.sharding import PartitionSpec as P

smooth_width = 3.0 / 8192.0
grid_middle = 2048.0
grid_step = 3.0 / 2048.0
base_levels = 16
first_kept = 4


def design(covariate_codes):
    level_codes = jnp.arange(base_levels, dtype=jnp.int32)
    kept_levels = jnp.arange(first_kept, base_levels, dtype=jnp.int32)
    groups = [covariate_codes[0][None, :] == level_codes[:, None]]
    for variable in range(1, covariate_codes.shape[0]):
        groups.append(covariate_codes[variable][None, :] == kept_levels[:, None])
    return jnp.concatenate(groups, axis=0).astype(jnp.float32)


def solve_controls(gram_sums, totals, controls):
    factor = jnp.linalg.cholesky(gram_sums)
    gap = (controls[None, :] - totals)[:, :, None]
    middle = lax.linalg.triangular_solve(factor, gap, left_side=True, lower=True)
    result = lax.linalg.triangular_solve(
        factor, middle, left_side=True, lower=True, transpose_a=True
    )
    return result[:, :, 0]


def shards(rep_weights, covariate_codes, tract_of, log_income, controls, threshold_grid):
    rep_count, row_count = rep_weights.shape
    ctrl_count = controls.shape[0]
    tract_count = lax.axis_size("tract")
    rec_count = lax.axis_size("rec")
    design_rows = design(covariate_codes)
    block_rows = math.gcd(row_count, 256)

    def gram_step(position, running):
        weight_block = lax.dynamic_slice_in_dim(rep_weights, position * block_rows, block_rows, 1)
        design_block = lax.dynamic_slice_in_dim(design_rows, position * block_rows, block_rows, 1)
        spread = (weight_block[:, None, :] * design_block[None, :, :]).reshape(
            rep_count * ctrl_count, block_rows
        )
        product = jnp.einsum("an,cn->ac", spread, design_block, precision=lax.Precision.HIGHEST)
        return running + product.reshape(rep_count, ctrl_count, ctrl_count)

    gram_sums = lax.fori_loop(
        0,
        row_count // block_rows,
        gram_step,
        jnp.zeros((rep_count, ctrl_count, ctrl_count), jnp.float32),
    )
    totals = jnp.einsum("rn,cn->rc", rep_weights, design_rows, precision=lax.Precision.HIGHEST)
    gram_sums, totals = lax.psum((gram_sums, totals), ("rec", "tract"))
    multipliers = solve_controls(gram_sums, totals, controls)
    factors = 1.0 + jnp.dot(multipliers, design_rows, precision=lax.Precision.HIGHEST)
    calibrated = rep_weights * factors
    sent_weights = calibrated.astype(jnp.bfloat16)
    centers = (threshold_grid.astype(jnp.float32) - grid_middle) * grid_step
    tract_ids = tract_of[:, 0]
    per_tract = float(row_count * rec_count)
    capacity = 3 * row_count // tract_count
    belongs = (tract_ids[:, None] == jnp.arange(tract_count, dtype=jnp.int32)[None, :]).astype(
        jnp.int32
    )
    earlier = jnp.cumsum(belongs, axis=0) - belongs
    slot_index = jnp.sum(earlier * belongs, axis=1)
    target = tract_ids * capacity + slot_index
    source = jnp.full((tract_count * capacity,), row_count, jnp.int32)
    source = source.at[target].set(jnp.arange(row_count, dtype=jnp.int32))
    payload = jnp.concatenate([sent_weights, log_income[None, :]], axis=0)
    payload = jnp.concatenate([payload, jnp.zeros((rep_count + 1, 1), jnp.bfloat16)], axis=1)
    buffer = jnp.take(payload, source.reshape(tract_count, capacity), axis=1)
    received = lax.all_to_all(buffer, "tract", split_axis=1, concat_axis=1, tiled=True)
    recv_weights = received[:rep_count]
    recv_income = received[rep_count].astype(jnp.float32)
    smoothed = jax.nn.sigmoid((centers[None, None, :] - recv_income[:, :, None]) / smooth_width)
    smoothed = smoothed.astype(jnp.bfloat16)
    term = lax.psum_scatter(
        jnp.einsum("rsm,smj->jr", recv_weights, smoothed, preferred_element_type=jnp.float32),
        "rec",
        scatter_dimension=0,
        tiled=True,
    )
    income_tables = (term.T / per_tract)[None]
    return (calibrated, income_tables)


def solution(mesh):
    placed = (
        P(None, ("rec", "tract")),
        P(None, ("rec", "tract")),
        P(("rec", "tract"), None),
        P(("rec", "tract")),
        P(),
        P(),
    )
    return jax.shard_map(
        shards,
        mesh=mesh,
        in_specs=placed,
        out_specs=(P(None, ("rec", "tract")), P("tract", None, "rec")),
        check_vma=False,
    )
```

profile of v0, /device:TPU:0, one launch (start us, length us, event | category | flops | bytes accessed | tf_op | source)
XLA Modules:
  0.0 996.2 jit_solution(17329571507120278312)
XLA Ops:
  7.2 1.5 fusion.21
  9.0 13.0 %concatenate.9 = pred[64,4096]{1,0:T(32,128)(4,1)S(1)} concatenate(pred[16,4096]{1,0:T(8,128)(4,1)S(1)} %iota_compare_fusion, pred[12,4096]{1,0:T(8,128)(4,1)S(1)} %get-tuple-element.113, pred[12,4096]{1,0:T(8,128)(4,1)S(1)} %get-tuple-element.111, pred[12,4096]{1,0:T(8,128)(4,1)S(1)} %get-tuple-element.112, pred[12,4096]{1,0:T(8,128)(4,1)S(1)} %get-tuple-element.110), dimensions={0} | concatenate | bytes 524288 | tf_op jit(solution)/shard_map/concatenate | solution.py:20
  22.0 1.1 convert_element_type.29
  23.1 109.5 %while.14 = (s32[]{:T(128)}, f32[80,64,64]{2,1,0:T(8,128)S(1)}, f32[80,4096]{1,0:T(8,128)}, f32[64,4096]{1,0:T(8,128)}, s32[]{:T(128)}, /*index=5*/s32[]{:T(128)}, s32[]{:T(128)}, s32[]{:T(128)}) while((s32[]{:T(128)}, f32[80,64,64]{2,1,0:T(8,128)S(1)}, f32[80,4096]{1,0:T(8,128)}, f32[64,4096]{1,0:T(8,128)}, s32[]{:T(128)}, ...), condition=%wide.region_1.0_spmd.clone, body=%wide.region_0.0_spmd.clone.sunk | while | flops 1008599040 | bytes 3063957 | solution.py:50
  24.9 5.1 select_add_fusion.2
  30.0 0.9 constant_dynamic-slice_fusion.5
  31.7 5.1 select_add_fusion.2
  36.8 0.9 constant_dynamic-slice_fusion.5
  38.6 5.1 select_add_fusion.2
  43.7 0.9 constant_dynamic-slice_fusion.5
  45.4 5.1 select_add_fusion.2
  52.3 5.1 select_add_fusion.2
  57.4 0.9 constant_dynamic-slice_fusion.5
  59.1 5.1 select_add_fusion.2
  66.0 5.1 select_add_fusion.2
  72.8 5.1 select_add_fusion.2
  79.7 5.1 select_add_fusion.2
  86.5 5.1 select_add_fusion.2
  93.4 5.1 select_add_fusion.2
  100.2 5.1 select_add_fusion.2
  107.0 5.1 select_add_fusion.2
  113.9 5.1 select_add_fusion.2
  120.7 5.1 select_add_fusion.2
  127.6 5.1 select_add_fusion.2
  132.7 2.1 copy.20
  134.9 1.2 copy-done.2
  137.0 2.3 reduce-window.6
  140.1 15.5 %scatter_custom_fusion = s32[12288]{0:T(1024)S(1)} fusion(s32[4096]{0:T(1024)S(1)} %bitcast.84, s32[4096]{0:T(1024)S(1)} %iota.52, s32[]{:T(128)} %constant.113.clone.1), kind=kCustom, calls=%fused_computation.50 | custom fusion | bytes 49156 | tf_op jit(solution)/shard_map/scatter | solution.py:73
  155.6 42.5 %psum.15 = f32[80,64]{0,1:T(8,128)S(1)} all-reduce(f32[80,64]{0,1:T(8,128)S(1)} %convolution_bitcast_fusion), channel_id=1, replica_groups=mesh['rec'=4,'tract'=8] {'rec','tract'}, use_global_device_ids=true, to_apply=%region_5.6 | all-reduce | flops 5120 | bytes 40960 | tf_op jit(solution)/shard_map/psum | solution.py:57
  198.3 75.6 %all-reduce.3.cloned.1.call-done = f32[80,64,64]{1,2,0:T(8,128)} async-done(((f32[80,64,64]{1,2,0:T(8,128)}), f32[80,64,64]{1,2,0:T(8,128)}) %all-reduce.3.cloned.1.call-update) | async-done | bytes 1310736 | tf_op jit(solution)/shard_map/psum | solution.py:57
  273.9 3.4 copy.21
  277.3 3.8 fusion.9
  281.1 470.7 %custom-call.9 = f32[80,64,64]{2,1,0:T(8,128)} custom-call(f32[80,64,64]{2,1,0:T(8,128)} %fusion.9), custom_call_target="Cholesky" | custom-call | tf_op jit(solution)/shard_map/jit(cholesky)/cholesky | solution.py:24
  751.8 2.7 copy.22
  755.3 1.7 select_bitcast_fusion.1
  757.0 67.2 %custom-call.10 = f32[80,1,64,64]{0,2,3,1:T(8,128)S(1)} custom-call(f32[80,1,64,64]{0,3,2,1:T(8,128)} %select_bitcast_fusion.1), custom_call_target="InvertDiagBlocksLowerTriangular" | custom-call | tf_op jit(solution)/shard_map/triangular_solve | solution.py:27
  824.6 1.0 copy-done.1
  825.6 3.6 copy.33
  829.2 4.2 fusion.23
  833.4 1.8 fusion.22
  836.2 43.3 %gather_fusion = bf16[12288,81]{1,0:T(8,128)(2,1)} fusion(bf16[81,4097]{0,1:T(8,128)(2,1)S(1)} %concatenate.11.clone, s32[12288]{0:T(1024)S(1)} %broadcast_clamp_fusion), kind=kCustom, calls=%fused_computation | custom fusion | bytes 4030464 | tf_op jit(solution)/shard_map/jit(_take)/gather | solution.py:76
  879.5 3.3 copy.26
  882.8 1.6 select_bitcast_fusion
  884.4 4.0 all-to-all-start
  888.5 48.2 %all-to-all-done = bf16[81,8,1536]{2,0,1:T(8,128)(2,1)S(1)} async-done(((bf16[81,8,1536]{2,0,1:T(8,128)(2,1)}), bf16[81,8,1536]{2,0,1:T(8,128)(2,1)S(1)}, u32[]{:S(2)}, u32[]{:S(2)}) %all-to-all-start) | async-done | bytes 1990688 | tf_op jit(solution)/shard_map/all_to_all | solution.py:77
  936.7 29.7 %fusion.10 = f32[2048,80]{0,1:T(8,128)} fusion(f32[8,1536]{1,0:T(8,128)S(1)} %bitcast.82, f32[2048]{0:T(1024)S(1)} %add_multiply_fusion, bf16[81,8,1536]{2,0,1:T(8,128)(2,1)S(1)} %all-to-all-done), kind=kOutput, calls=%fused_computation.16 | convolution fusion | flops 4177526784 | bytes 2678784 | tf_op jit(solution)/shard_map/rsm,smj->jr/dot_general | solution.py:83
  966.4 21.3 %reduce-scatter.2.cloned.1.call-done = f32[512,80]{0,1:T(8,128)} async-done(((f32[2048,80]{0,1:T(8,128)}), f32[512,80]{0,1:T(8,128)}) %reduce-scatter.2.cloned.1.call-update) | async-done | bytes 163856 | tf_op jit(solution)/shard_map/reduce_scatter | solution.py:82
  987.8 1.6 multiply_bitcast_fusion
  (78 shorter events, 28.5 us)
Async XLA Ops:
  7.2 266.7 %all-reduce.3.cloned.1.call-start = ((), (), s32[]{:S(2)}) async-start(), calls=%async_computation.2 | async-start | bytes 5242880 | tf_op jit(solution)/shard_map/psum | solution.py:57
  134.8 1.3 copy-start.2
  134.8 2.1 copy-start.4
  134.8 63.3 %copy-start.5 = (bf16[4096]{0:T(1024)(128)(2,1)S(1)}, bf16[4096]{0:T(1024)(128)(2,1)}, u32[]{:S(2)}) copy-start(bf16[4096]{0:T(1024)(128)(2,1)} %param.11) | copy-start | bytes 24580
  134.8 63.4 %copy-start.7 = (f32[64]{0:T(128)S(1)}, f32[64]{0:T(128)}, u32[]{:S(2)}) copy-start(f32[64]{0:T(128)} %param.12) | copy-start | bytes 772
  273.9 3.4 copy-start
  824.3 1.4 copy-start.1
  829.2 4.2 copy-start.3
  884.4 4.1 copy-start.6
  884.4 52.3 %all-to-all-start = ((bf16[81,8,1536]{2,0,1:T(8,128)(2,1)}), bf16[81,8,1536]{2,0,1:T(8,128)(2,1)S(1)}, u32[]{:S(2)}, u32[]{:S(2)}) async-start(bf16[81,8,1536]{2,0,1:T(8,128)(2,1)} %select_bitcast_fusion), calls=%async_computation | async-start | bytes 4325376 | tf_op jit(solution)/shard_map/all_to_all | solution.py:77
  888.4 99.3 %reduce-scatter.2.cloned.1.call-start = ((), (), s32[]{:S(2)}) async-start(), calls=%async_computation.3 | async-start | bytes 819200 | tf_op jit(solution)/shard_map/reduce_scatter | solution.py:82
Sparse Core Ops, SparseCore 0:
  135.0 138.9 all-reduce.2
  966.5 21.1 reduce-scatter.1
where the time goes:
time: 998 us; the launch traced here: 996 us
  other arithmetic  552 us (55%)
  waiting for transfers between devices  145 us (15%)
  local copies, waits for them, and re-layouts  120 us (12%)
  matrix products  118 us (12%)
  blocking collectives  42.5 us (4%)
  between operations  14.4 us (1%)
    another operation x4, other arithmetic, solve_controls(): factor = jnp.linalg.cholesky(gram_sums)  471 us
    dot_general x16, matrix products, gram_step(): jnp.einsum('an,cn->ac', spread, design_block, precision=lax.Precision.HIG...  81.2 us
    psum x1, waiting for transfers between devices, shards(): gram_sums, totals = lax.psum((gram_sums, totals), ('rec', 'tract'))  75.6 us
    another operation x3, other arithmetic, solve_controls(): lax.linalg.triangular_solve(factor, middle, left_side=True, lower=True, t...  69 us
    all_to_all x1, waiting for transfers between devices, shards(): lax.all_to_all(buffer, 'tract', split_axis=1, concat_axis=1, tiled=True)  48.2 us
    gather x2, local copies, waits for them, and re-layouts, shards(): buffer = jnp.take(payload, source.reshape(tract_count, capacity), axis=1)  46.6 us
    psum x1, blocking collectives, shards(): gram_sums, totals = lax.psum((gram_sums, totals), ('rec', 'tract'))  42.5 us
    dot_general x1, matrix products, shards(): jnp.einsum('rsm,smj->jr', recv_weights, smoothed, preferred_element_type=...  29.7 us
  transfers between devices with their start and end apart: 3, of which 3 were waited for; matrix products, arithmetic and copies ran while one was open for 2% of the time, Pallas kernels for 0%

commit v1 on v0

--- a/solution.py
+++ b/solution.py
@@ -31,6 +31,11 @@
 
 
 def shards(rep_weights, covariate_codes, tract_of, log_income, controls, threshold_grid):
+
+    def answer_numbers(local_array, device_axis, shard_axis):
+        y2 = lax.psum(lax.psum(local_array, device_axis), shard_axis)
+        return y2
+
     rep_count, row_count = rep_weights.shape
     ctrl_count = controls.shape[0]
     tract_count = lax.axis_size("tract")
@@ -54,7 +59,7 @@
         jnp.zeros((rep_count, ctrl_count, ctrl_count), jnp.float32),
     )
     totals = jnp.einsum("rn,cn->rc", rep_weights, design_rows, precision=lax.Precision.HIGHEST)
-    gram_sums, totals = lax.psum((gram_sums, totals), ("rec", "tract"))
+    gram_sums, totals = answer_numbers((gram_sums, totals), "tract", "rec")
     multipliers = solve_controls(gram_sums, totals, controls)
     factors = 1.0 + jnp.dot(multipliers, design_rows, precision=lax.Precision.HIGHEST)
     calibrated = rep_weights * factors

time: 998 us -> 1040 us (1.042)
  waiting for transfers between devices: 145 us -> 181 us
    psum x1 -> x2, waiting for transfers between devices: 75.6 us -> 110 us  [answer_numbers(): y2 = lax.psum(lax.psum(local_array, device_axis), shard_axis)]
    psum x1 -> x2, blocking collectives: 42.5 us -> 50.1 us  [answer_numbers(): y2 = lax.psum(lax.psum(local_array, device_axis), shard_axis)]
  transfers between devices with their start and end apart: 3 -> 4, of which waited for: 3 -> 4; matrix products, arithmetic and copies ran while one was open for 2% -> 2% of each run, Pallas kernels for 0% -> 0%
where the time goes in v1:
time: 1040 us
  other arithmetic  552 us (53%)
  waiting for transfers between devices  181 us (17%)
  local copies, waits for them, and re-layouts  119 us (11%)
  matrix products  118 us (11%)
  blocking collectives  50.1 us (5%)
  between operations  14.1 us (1%)
    another operation x4, other arithmetic, solve_controls(): factor = jnp.linalg.cholesky(gram_sums)  471 us
    psum x2, waiting for transfers between devices, answer_numbers(): y2 = lax.psum(lax.psum(local_array, device_axis), shard_axis)  110 us
    dot_general x16, matrix products, gram_step(): jnp.einsum('an,cn->ac', spread, design_block, precision=lax.Precision.HIG...  81.2 us
    another operation x3, other arithmetic, solve_controls(): lax.linalg.triangular_solve(factor, middle, left_side=True, lower=True, t...  69 us
    psum x2, blocking collectives, answer_numbers(): y2 = lax.psum(lax.psum(local_array, device_axis), shard_axis)  50.1 us
    all_to_all x1, waiting for transfers between devices, shards(): lax.all_to_all(buffer, 'tract', split_axis=1, concat_axis=1, tiled=True)  49.5 us
    gather x2, local copies, waits for them, and re-layouts, shards(): buffer = jnp.take(payload, source.reshape(tract_count, capacity), axis=1)  46.6 us
    dot_general x1, matrix products, shards(): jnp.einsum('rsm,smj->jr', recv_weights, smoothed, preferred_element_type=...  29.7 us
  transfers between devices with their start and end apart: 4, of which 4 were waited for; matrix products, arithmetic and copies ran while one was open for 2% of the time, Pallas kernels for 0%

profile of v1, /device:TPU:0, one launch (start us, length us, event | category | flops | bytes accessed | tf_op | source)
XLA Modules:
  0.0 1040.1 jit_solution(11303547499726919429)
XLA Ops:
  7.2 1.5 fusion.21
  9.0 13.0 %concatenate.9 = pred[64,4096]{1,0:T(32,128)(4,1)S(1)} concatenate(pred[16,4096]{1,0:T(8,128)(4,1)S(1)} %iota_compare_fusion, pred[12,4096]{1,0:T(8,128)(4,1)S(1)} %get-tuple-element.113, pred[12,4096]{1,0:T(8,128)(4,1)S(1)} %get-tuple-element.111, pred[12,4096]{1,0:T(8,128)(4,1)S(1)} %get-tuple-element.112, pred[12,4096]{1,0:T(8,128)(4,1)S(1)} %get-tuple-element.110), dimensions={0} | concatenate | bytes 524288 | tf_op jit(solution)/shard_map/concatenate | solution.py:20
  22.0 1.1 convert_element_type.29
  23.1 109.5 %while.14 = (s32[]{:T(128)}, f32[80,64,64]{2,1,0:T(8,128)S(1)}, f32[80,4096]{1,0:T(8,128)}, f32[64,4096]{1,0:T(8,128)}, s32[]{:T(128)}, /*index=5*/s32[]{:T(128)}, s32[]{:T(128)}, s32[]{:T(128)}) while((s32[]{:T(128)}, f32[80,64,64]{2,1,0:T(8,128)S(1)}, f32[80,4096]{1,0:T(8,128)}, f32[64,4096]{1,0:T(8,128)}, s32[]{:T(128)}, ...), condition=%wide.region_1.0_spmd.clone, body=%wide.region_0.0_spmd.clone.sunk | while | flops 1008599040 | bytes 3063957 | solution.py:55
  24.9 5.1 select_add_fusion.2
  30.0 0.9 constant_dynamic-slice_fusion.5
  31.7 5.1 select_add_fusion.2
  36.8 0.9 constant_dynamic-slice_fusion.5
  38.6 5.1 select_add_fusion.2
  45.4 5.1 select_add_fusion.2
  52.3 5.1 select_add_fusion.2
  57.4 0.9 constant_dynamic-slice_fusion.5
  59.1 5.1 select_add_fusion.2
  66.0 5.1 select_add_fusion.2
  72.8 5.1 select_add_fusion.2
  79.7 5.1 select_add_fusion.2
  86.5 5.1 select_add_fusion.2
  93.4 5.1 select_add_fusion.2
  100.2 5.1 select_add_fusion.2
  107.0 5.1 select_add_fusion.2
  113.9 5.1 select_add_fusion.2
  120.7 5.1 select_add_fusion.2
  127.6 5.1 select_add_fusion.2
  132.7 2.1 copy.20
  135.5 2.3 reduce-window.6
  138.6 15.5 %scatter_custom_fusion = s32[12288]{0:T(1024)S(1)} fusion(s32[4096]{0:T(1024)S(1)} %bitcast.84, s32[4096]{0:T(1024)S(1)} %iota.52, s32[]{:T(128)} %constant.113.clone.1), kind=kCustom, calls=%fused_computation.50 | custom fusion | bytes 49156 | tf_op jit(solution)/shard_map/scatter | solution.py:78
  155.1 39.6 %psum.30 = f32[80,64]{0,1:T(8,128)S(1)} all-reduce(f32[80,64]{0,1:T(8,128)S(1)} %convolution_bitcast_fusion), channel_id=1, replica_groups=mesh['rec'=4,'tract'=8] {'tract'}, use_global_device_ids=true, to_apply=%region_6.7 | all-reduce | flops 5120 | bytes 40960 | tf_op jit(solution)/shard_map/psum | solution.py:36
  194.7 10.4 %psum.31 = f32[80,64]{0,1:T(8,128)S(1)} all-reduce(f32[80,64]{0,1:T(8,128)S(1)} %psum.30), channel_id=1, replica_groups=mesh['rec'=4,'tract'=8] {'rec'}, use_global_device_ids=true, to_apply=%region_7.8 | all-reduce | flops 5120 | bytes 40960 | tf_op jit(solution)/shard_map/psum | solution.py:36
  205.2 48.7 %all-reduce.4.cloned.1.call-done = f32[80,64,64]{1,2,0:T(8,128)} async-done(((f32[80,64,64]{1,2,0:T(8,128)}), f32[80,64,64]{1,2,0:T(8,128)}) %all-reduce.4.cloned.1.call-update) | async-done | bytes 1310736 | tf_op jit(solution)/shard_map/psum | solution.py:36
  254.1 61.2 %all-reduce.6.cloned.1.call-done = f32[80,64,64]{1,2,0:T(8,128)} async-done(((f32[80,64,64]{1,2,0:T(8,128)}), f32[80,64,64]{1,2,0:T(8,128)}) %all-reduce.6.cloned.1.call-update) | async-done | bytes 1310736 | tf_op jit(solution)/shard_map/psum | solution.py:36
  315.3 3.4 copy.21
  318.7 4.1 fusion.9
  322.8 470.6 %custom-call.9 = f32[80,64,64]{2,1,0:T(8,128)} custom-call(f32[80,64,64]{2,1,0:T(8,128)} %fusion.9), custom_call_target="Cholesky" | custom-call | tf_op jit(solution)/shard_map/jit(cholesky)/cholesky | solution.py:24
  793.4 2.7 copy.22
  796.9 1.7 select_bitcast_fusion.1
  798.6 67.2 %custom-call.10 = f32[80,1,64,64]{0,2,3,1:T(8,128)S(1)} custom-call(f32[80,1,64,64]{0,3,2,1:T(8,128)} %select_bitcast_fusion.1), custom_call_target="InvertDiagBlocksLowerTriangular" | custom-call | tf_op jit(solution)/shard_map/triangular_solve | solution.py:27
  866.2 1.0 copy-done.1
  867.3 3.6 copy.33
  870.8 4.2 fusion.23
  875.0 1.8 fusion.22
  877.8 43.3 %gather_fusion = bf16[12288,81]{1,0:T(8,128)(2,1)} fusion(bf16[81,4097]{0,1:T(8,128)(2,1)S(1)} %concatenate.11.clone, s32[12288]{0:T(1024)S(1)} %broadcast_clamp_fusion), kind=kCustom, calls=%fused_computation | custom fusion | bytes 4030464 | tf_op jit(solution)/shard_map/jit(_take)/gather | solution.py:81
  921.2 3.3 copy.26
  924.5 1.6 select_bitcast_fusion
  926.1 5.6 all-to-all-start
  931.8 49.5 %all-to-all-done = bf16[81,8,1536]{2,0,1:T(8,128)(2,1)S(1)} async-done(((bf16[81,8,1536]{2,0,1:T(8,128)(2,1)}), bf16[81,8,1536]{2,0,1:T(8,128)(2,1)S(1)}, u32[]{:S(2)}, u32[]{:S(2)}) %all-to-all-start) | async-done | bytes 1990688 | tf_op jit(solution)/shard_map/all_to_all | solution.py:82
  981.3 29.7 %fusion.10 = f32[2048,80]{0,1:T(8,128)} fusion(f32[8,1536]{1,0:T(8,128)S(1)} %bitcast.82, f32[2048]{0:T(1024)S(1)} %add_multiply_fusion, bf16[81,8,1536]{2,0,1:T(8,128)(2,1)S(1)} %all-to-all-done), kind=kOutput, calls=%fused_computation.16 | convolution fusion | flops 4177526784 | bytes 2678784 | tf_op jit(solution)/shard_map/rsm,smj->jr/dot_general | solution.py:88
  1011.0 21.0 %reduce-scatter.2.cloned.1.call-done = f32[512,80]{0,1:T(8,128)} async-done(((f32[2048,80]{0,1:T(8,128)}), f32[512,80]{0,1:T(8,128)}) %reduce-scatter.2.cloned.1.call-update) | async-done | bytes 163856 | tf_op jit(solution)/shard_map/reduce_scatter | solution.py:87
  1032.0 1.6 multiply_bitcast_fusion
  (82 shorter events, 30.1 us)
Async XLA Ops:
  7.2 246.8 %all-reduce.4.cloned.1.call-start = ((), (), s32[]{:S(2)}) async-start(), calls=%async_computation.2 | async-start | bytes 5242880 | tf_op jit(solution)/shard_map/psum | solution.py:36
  134.8 0.7 copy-start.4
  134.8 19.4 %copy-start.5 = (bf16[4096]{0:T(1024)(128)(2,1)S(1)}, bf16[4096]{0:T(1024)(128)(2,1)}, u32[]{:S(2)}) copy-start(bf16[4096]{0:T(1024)(128)(2,1)} %param.11) | copy-start | bytes 24580
  134.8 19.5 %copy-start.2 = (f32[80,4096]{1,0:T(8,128)S(1)}, f32[80,4096]{1,0:T(8,128)}, u32[]{:S(2)}) copy-start(f32[80,4096]{1,0:T(8,128)} %get-tuple-element.171) | copy-start | bytes 3932164
  134.8 180.5 %all-reduce.6.cloned.1.call-start = ((), (), s32[]{:S(2)}) async-start(), calls=%async_computation.3 | async-start | bytes 5242880 | tf_op jit(solution)/shard_map/psum | solution.py:36
  138.5 115.5 %copy-start.7 = (f32[64]{0:T(128)S(1)}, f32[64]{0:T(128)}, u32[]{:S(2)}) copy-start(f32[64]{0:T(128)} %param.12) | copy-start | bytes 772
  315.3 3.4 copy-start
  865.9 1.4 copy-start.1
  870.8 4.2 copy-start.3
  926.1 5.7 copy-start.6
  926.1 55.2 %all-to-all-start = ((bf16[81,8,1536]{2,0,1:T(8,128)(2,1)}), bf16[81,8,1536]{2,0,1:T(8,128)(2,1)S(1)}, u32[]{:S(2)}, u32[]{:S(2)}) async-start(bf16[81,8,1536]{2,0,1:T(8,128)(2,1)} %select_bitcast_fusion), calls=%async_computation | async-start | bytes 4325376 | tf_op jit(solution)/shard_map/all_to_all | solution.py:82
  931.7 100.3 %reduce-scatter.2.cloned.1.call-start = ((), (), s32[]{:S(2)}) async-start(), calls=%async_computation.4 | async-start | bytes 819200 | tf_op jit(solution)/shard_map/reduce_scatter | solution.py:87
Sparse Core Ops, SparseCore 0:
  135.0 118.9 all-reduce.3
  256.3 58.9 all-reduce.5
  1011.1 20.8 reduce-scatter.1
